TPU v7x, 128 devices: a whole 4x4x4 slice. The times are simulated.
128 devices in a mesh: chan: 16 (over y, x), tm: 8 (over z, core).
Axes of the slice: x: 4, y: 4, z: 4, core: 2. Of those that a mesh axis runs over, the one named last changes fastest.
Arguments:
- samples: bfloat16 [256, 192, 4096], P('chan', 'tm'), may hold values from -6 to 6
- taps: float32 [16, 4096], replicated, may hold values from -1.5 to 1.5
- block_tile: int32 [120], replicated, may hold values from 0 to 15, as said below
- tile_slots: int32 [16], replicated, may hold values from 0 to 15, as said below
- kern_u: bfloat16 [16, 30720], replicated, may hold values from -1.1953125 to 1.1953125
- kern_v: bfloat16 [16, 30720], replicated, may hold values from -1.1953125 to 1.1953125
Outputs:
- uv_grid: float32 [16, 2048, 2, 256], P('tm', 'chan')
Inputs may be any that keep to these rules, and one draw needn't show every extreme that they name: `block_tile`: A tile's owner is (its position in tile_slots) // 2. The blocks that fall in the tiles of one owner are at most 30; in every draw one owner has exactly 30. `tile_slots`: each tile number stands once.
All inputs are finite; a program needn't handle non-finite values.
Results may differ from a plain program's by a relative error of at most 0.0077.
Values may be sent and summed in bfloat16 or wider, within the bound.
No kernel may reach another device: no remote copies, remote signals or barrier semaphores. Data moves between devices by JAX's collectives and lax.ppermute only.
A program may use at most 192 MiB of HBM per device.

v0:
```python
import math
import jax
import jax.numpy as jnp
import numpy as np
from jax import lax
from jax.sharding import PartitionSpec as P

SBLK = 16
GRID = 16


def passed_along(value, axis, steps):
    count = lax.axis_size(axis)
    leading, last = (max(0, -steps), min(count, count - steps))
    return lax.ppermute(value, axis, [(source, source + steps) for source in range(leading, last)])


def block_pairs(block_total):
    left_list = []
    right_list = []
    for p in range(block_total):
        for q in range(p + 1, block_total):
            left_list.append(p)
            right_list.append(q)
    return (np.array(left_list, dtype=np.int32), np.array(right_list, dtype=np.int32))


def make_kernel(u_part, v_part, block_total):
    u_cols = u_part.astype(jnp.float32).reshape(GRID, block_total, SBLK * SBLK).transpose(1, 2, 0)
    v_cols = v_part.astype(jnp.float32).reshape(GRID, block_total, SBLK * SBLK).transpose(1, 2, 0)
    product = u_cols[:, :, :, None] * v_cols[:, :, None, :]
    return product.reshape(block_total, SBLK * SBLK, GRID * GRID).astype(jnp.bfloat16)


def body(samples, taps, block_tile, tile_slots, kern_u, kern_v):
    station_count, frame_count, length = samples.shape
    channel_count = length // 2
    chan_size = lax.axis_size("chan")
    tm_size = lax.axis_size("tm")
    group_count = chan_size * tm_size
    group_width = channel_count // group_count
    tap_count = taps.shape[0]
    history = passed_along(samples[:, frame_count - (tap_count - 1) :], "tm", 1)
    padded = jnp.concatenate([history, samples], axis=1)
    filtered = jnp.zeros((station_count, frame_count, length), jnp.float32)
    for tap_index in range(tap_count):
        offset = tap_count - 1 - tap_index
        filtered = filtered + taps[tap_index] * padded[:, offset : offset + frame_count].astype(
            jnp.float32
        )
    rows_in = filtered.astype(jnp.bfloat16).reshape(station_count * frame_count, length)
    dft_scale = 1.0 / math.sqrt(length)
    block_cols = min(channel_count, 256)
    groups_per_block = block_cols // group_width
    positions = jnp.arange(length, dtype=jnp.int32)[:, None, None]
    pieces = []
    for column_block in range(channel_count // block_cols):
        channels = column_block * block_cols + jnp.arange(block_cols, dtype=jnp.int32).reshape(
            1, groups_per_block, group_width
        )
        phase_int = positions * channels % length
        phase_angle = phase_int.astype(jnp.float32) * (2.0 * math.pi / length)
        cosine = jnp.cos(phase_angle).astype(jnp.bfloat16)
        sine_neg = (-jnp.sin(phase_angle)).astype(jnp.bfloat16)
        dft_table = jnp.stack([cosine, sine_neg], axis=2).reshape(length, 2 * block_cols)
        spectrum = (
            lax.dot_general(
                dft_table, rows_in, (((0,), (1,)), ((), ())), preferred_element_type=jnp.float32
            )
            * dft_scale
        )
        pieces.append(
            spectrum.astype(jnp.bfloat16).reshape(
                groups_per_block, 2, group_width, station_count, frame_count
            )
        )
    spectra = jnp.concatenate(pieces, axis=0)
    stations = station_count * chan_size
    frames = frame_count * tm_size
    arranged = spectra.reshape(chan_size, tm_size, 2, group_width, station_count, frame_count)
    turned = lax.all_to_all(
        lax.all_to_all(arranged, "chan", split_axis=0, concat_axis=4, tiled=True),
        "tm",
        split_axis=1,
        concat_axis=5,
        tiled=True,
    )
    turned = turned.reshape(2, group_width, stations, frames)
    block_rows = stations // SBLK
    block_total = block_rows * (block_rows - 1) // 2
    vis_scale = 1.0 / math.sqrt(frames)
    swapped = jnp.stack([turned[1], -turned[0]], axis=0)
    real_part = (
        jnp.einsum("cgib,cgjb->gij", turned, turned, preferred_element_type=jnp.float32) * vis_scale
    )
    imag_part = (
        jnp.einsum("cgib,cgjb->gij", swapped, turned, preferred_element_type=jnp.float32)
        * vis_scale
    )
    left_idx, right_idx = block_pairs(block_rows)
    visibility = jnp.stack([real_part, imag_part], axis=1).reshape(
        group_width, 2, block_rows, SBLK, block_rows, SBLK
    )
    visibility = visibility[:, :, left_idx, :, right_idx, :]
    blocks = visibility.reshape(block_total, group_width, 2, SBLK * SBLK).astype(jnp.bfloat16)
    tile_count = tile_slots.shape[0]
    slot_ids = jnp.arange(tile_count, dtype=jnp.int32)
    tile_match = block_tile[:, None] == tile_slots[None, :]
    slot_of_block = jnp.sum(jnp.where(tile_match, slot_ids[None, :], 0), axis=1)
    kernel = make_kernel(kern_u, kern_v, block_total)
    per_block = jnp.einsum("mgce,mel->mgcl", blocks, kernel, preferred_element_type=jnp.float32)
    slot_hits = (slot_of_block[:, None] == slot_ids[None, :]).astype(jnp.float32)
    partial_value = jnp.einsum(
        "mgcl,ms->sgcl", per_block, slot_hits, precision=lax.Precision.HIGHEST
    )
    uv_grid = lax.all_to_all(partial_value, "tm", split_axis=0, concat_axis=1, tiled=True)
    return uv_grid


def solution(mesh):
    placed = (P("chan", "tm", None), P(), P(), P(), P(), P())
    return jax.shard_map(
        body, mesh=mesh, in_specs=placed, out_specs=P("tm", "chan", None, None), check_vma=False
    )
```

profile of v0, /device:TPU:1, one launch (start us, length us, event | category | flops | bytes accessed | tf_op | source)
XLA Modules:
  0.0 647.3 jit_solution(4451937538021533933)
XLA Ops:
  9.7 18.1 %cosine_convert_fusion.7 = (bf16[4096,16,1,16]{0,3,2,1:T(8,128)(2,1)S(1)}, bf16[4096,16,1,16]{0,3,2,1:T(8,128)(2,1)S(1)}) fusion(s32[16,16]{1,0:T(8,128)S(1)} %multiply_add_fusion), kind=kLoop, calls=%fused_computation.119 | loop fusion | flops 17825792 | bytes 4195328 | tf_op jit(solution)/shard_map/convert_element_type | solution.py:63
  27.7 18.1 %cosine_convert_fusion.6 = (bf16[4096,16,1,16]{0,3,2,1:T(8,128)(2,1)S(1)}, bf16[4096,16,1,16]{0,3,2,1:T(8,128)(2,1)S(1)}) fusion(s32[16,16]{1,0:T(8,128)S(1)} %fusion.84), kind=kLoop, calls=%fused_computation.115 | loop fusion | flops 17825792 | bytes 4195328 | tf_op jit(solution)/shard_map/convert_element_type | solution.py:63
  45.8 18.1 %cosine_convert_fusion.5 = (bf16[4096,16,1,16]{0,3,2,1:T(8,128)(2,1)S(1)}, bf16[4096,16,1,16]{0,3,2,1:T(8,128)(2,1)S(1)}) fusion(s32[16,16]{1,0:T(8,128)S(1)} %fusion.83), kind=kLoop, calls=%fused_computation.111 | loop fusion | flops 17825792 | bytes 4195328 | tf_op jit(solution)/shard_map/convert_element_type | solution.py:63
  63.9 18.1 %cosine_convert_fusion.4 = (bf16[4096,16,1,16]{0,3,2,1:T(8,128)(2,1)S(1)}, bf16[4096,16,1,16]{0,3,2,1:T(8,128)(2,1)S(1)}) fusion(s32[16,16]{1,0:T(8,128)S(1)} %fusion.82), kind=kLoop, calls=%fused_computation.107 | loop fusion | flops 17825792 | bytes 4195328 | tf_op jit(solution)/shard_map/convert_element_type | solution.py:63
  82.0 18.1 %cosine_convert_fusion.3 = (bf16[4096,16,1,16]{0,3,2,1:T(8,128)(2,1)S(1)}, bf16[4096,16,1,16]{0,3,2,1:T(8,128)(2,1)S(1)}) fusion(s32[16,16]{1,0:T(8,128)S(1)} %fusion.81), kind=kLoop, calls=%fused_computation.103 | loop fusion | flops 17825792 | bytes 4195328 | tf_op jit(solution)/shard_map/convert_element_type | solution.py:63
  100.0 18.1 %cosine_convert_fusion.2 = (bf16[4096,16,1,16]{0,3,2,1:T(8,128)(2,1)S(1)}, bf16[4096,16,1,16]{0,3,2,1:T(8,128)(2,1)S(1)}) fusion(s32[16,16]{1,0:T(8,128)S(1)} %fusion.80), kind=kLoop, calls=%fused_computation.99 | loop fusion | flops 17825792 | bytes 4195328 | tf_op jit(solution)/shard_map/convert_element_type | solution.py:63
  118.1 18.1 %cosine_convert_fusion.1 = (bf16[4096,16,1,16]{0,3,2,1:T(8,128)(2,1)S(1)}, bf16[4096,16,1,16]{0,3,2,1:T(8,128)(2,1)S(1)}) fusion(s32[16,16]{1,0:T(8,128)S(1)} %fusion.79), kind=kLoop, calls=%fused_computation.95 | loop fusion | flops 17825792 | bytes 4195328 | tf_op jit(solution)/shard_map/convert_element_type | solution.py:63
  136.2 19.0 %cosine_convert_fusion = (bf16[4096,16,1,16]{0,3,2,1:T(8,128)(2,1)S(1)}, bf16[4096,16,1,16]{0,3,2,1:T(8,128)(2,1)}) fusion(s32[16,16]{1,0:T(8,128)S(1)} %fusion.78), kind=kLoop, calls=%fused_computation.91 | loop fusion | flops 17825792 | bytes 4195328 | tf_op jit(solution)/shard_map/convert_element_type | solution.py:63
  178.3 23.2 %add_convert_fusion = bf16[16,24,4096]{2,1,0:T(8,128)(2,1)} fusion(bf16[16,24,4096]{2,1,0:T(8,128)(2,1)S(1)} %copy-done, bf16[16,15,4096]{2,1,0:T(8,128)(2,1)} %copy.81, f32[4096]{0:T(1024)S(1)} %bitcast.136, f32[4096]{0:T(1024)S(1)} %bitcast.137, f32[4096]{0:T(1024)S(1)} %bitcast.123, f32[4096]{0:T(1024)S(1)} %bitcast.124, f32[4096]{0:T(1024)S(1)} %bitcast.125, ...), kind=kLoop, calls=%fused_computation.52 | loop fusion | flops 146276352 | bytes 8519680 | tf_op jit(solution)/shard_map/convert_element_type | solution.py:51
  201.5 5.5 fusion.70
  220.1 5.5 fusion.72
  238.5 5.5 fusion.74
  247.8 5.5 fusion.75
  257.2 5.5 fusion.76
  266.4 5.5 fusion.77
  288.1 22.6 %reshape.779 = bf16[16,2,49152]{2,1,0:T(2,128)(2,1)S(1)} reshape(bf16[16,8,2,16,16,24]{5,4,3,2,1,0:T(8,128)(2,1)} %bitcast.96) | data formatting | bytes 6291456
  310.7 47.5 %all_to_all.51 = bf16[16,2,49152]{2,1,0:T(2,128)(2,1)} all-to-all(bf16[16,2,49152]{2,1,0:T(2,128)(2,1)S(1)} %reshape.779), channel_id=1, replica_groups=mesh['chan'=16,'tm'=8] {'chan'}, dimensions={0} | all-to-all | bytes 6291456 | tf_op jit(solution)/shard_map/all_to_all | solution.py:82
  358.2 25.0 %reshape.780 = bf16[16,8,2,16,16,24]{5,4,3,2,1,0:T(8,128)(2,1)} reshape(bf16[16,2,49152]{2,1,0:T(2,128)(2,1)} %all_to_all.51) | data formatting | bytes 6291456
  383.2 32.4 %copy.82 = bf16[1,8,2,16,16,16,24]{5,4,6,3,2,1,0:T(8,128)(2,1)} copy(bf16[1,8,2,16,16,16,24]{6,5,3,2,1,4,0:T(8,128)(2,1)} %bitcast.92) | data formatting | bytes 6291456 | tf_op jit(solution)/shard_map/all_to_all | solution.py:82
  415.6 30.1 %all_to_all.40 = bf16[1,8,2,16,256,24]{4,5,3,2,1,0:T(8,128)(2,1)} reshape(bf16[1,8,2,16,16,16,24]{5,4,6,3,2,1,0:T(8,128)(2,1)} %copy.82) | data formatting | bytes 6291456 | tf_op jit(solution)/shard_map/all_to_all | solution.py:82
  453.6 8.7 %multiply_convert_fusion = bf16[120,256,16,16]{1,3,2,0:T(8,128)(2,1)} fusion(f32[120,256,16]{1,2,0:T(8,128)S(1)} %get-tuple-element.39, f32[120,256,16]{1,2,0:T(8,128)S(1)} %get-tuple-element.40), kind=kLoop, calls=%fused_computation.2 | loop fusion | flops 15728640 | bytes 19660800 | tf_op jit(solution)/shard_map/convert_element_type | solution.py:32
  462.2 25.4 %all-to-all-done.1 = bf16[1,8,2,16,256,24]{4,5,3,2,0,1:T(8,128)(2,1)S(1)} async-done(((bf16[1,8,2,16,256,24]{4,5,3,2,0,1:T(8,128)(2,1)}), bf16[1,8,2,16,256,24]{4,5,3,2,0,1:T(8,128)(2,1)S(1)}, u32[]{:S(2)}, u32[]{:S(2)}) %all-to-all-start.1) | async-done | bytes 3145760 | tf_op jit(solution)/shard_map/all_to_all | solution.py:81
  492.8 17.4 %stack.63 = bf16[16,1,16,16,16,16]{5,4,3,2,0,1:T(8,128)(2,1)} reshape(bf16[16,256,256]{2,1,0:T(8,128)(2,1)} %bitcast_multiply_fusion) | data formatting | bytes 4194304 | tf_op jit(solution)/shard_map/stack | solution.py:101
  510.2 16.6 %copy.88 = bf16[16,1,16,16,16,16]{5,3,4,2,1,0:T(8,128)(2,1)} copy(bf16[16,1,16,16,16,16]{5,4,3,2,0,1:T(8,128)(2,1)} %stack.63) | data formatting | bytes 4194304 | tf_op jit(solution)/shard_map/stack | solution.py:101
  526.9 14.3 %stack.61 = bf16[16,1,16,16,16,16]{5,4,3,2,0,1:T(8,128)(2,1)} reshape(bf16[16,256,256]{2,1,0:T(8,128)(2,1)S(1)} %bitcast_multiply_fusion.1) | data formatting | bytes 4194304 | tf_op jit(solution)/shard_map/stack | solution.py:101
  541.2 16.6 %copy.87 = bf16[16,1,16,16,16,16]{5,3,4,2,1,0:T(8,128)(2,1)} copy(bf16[16,1,16,16,16,16]{5,4,3,2,0,1:T(8,128)(2,1)} %stack.61) | data formatting | bytes 4194304 | tf_op jit(solution)/shard_map/stack | solution.py:101
  557.8 22.7 %pad_maximum_fusion = bf16[16,2,16,16,16,16]{5,3,4,2,1,0:T(8,128)(2,1)} fusion(bf16[16,1,16,16,16,16]{5,3,4,2,1,0:T(8,128)(2,1)} %copy.88, bf16[16,1,16,16,16,16]{5,3,4,2,1,0:T(8,128)(2,1)} %copy.87), kind=kLoop, calls=%fused_computation.1 | loop fusion | flops 2097152 | bytes 8388608 | tf_op jit(solution)/shard_map/stack | solution.py:101
  580.5 12.2 %gather_fusion = bf16[120,16,2,16,16]{4,3,2,1,0:T(8,128)(2,1)} fusion(bf16[16,2,16,16,16,16]{5,3,4,2,1,0:T(8,128)(2,1)} %pad_maximum_fusion, s32[120]{0:T(128)S(1)} %copy-done.8), kind=kCustom, calls=%fused_computation | custom fusion | bytes 3933120 | tf_op jit(solution)/shard_map/gather | solution.py:104
  592.7 18.3 %copy.89 = bf16[120,16,2,16,16]{0,4,3,2,1:T(8,128)(2,1)S(1)} copy(bf16[120,16,2,16,16]{4,3,2,1,0:T(8,128)(2,1)} %gather_fusion) | data formatting | bytes 3932160 | tf_op jit(solution)/shard_map/gather | solution.py:104
  614.3 12.6 %fusion.91 = f32[120,16,2,256]{3,1,2,0:T(8,128)} fusion(bf16[120,16,2,256]{3,1,2,0:T(8,128)(2,1)} %copy.92, bf16[120,256,256,1]{1,2,3,0:T(8,128)(2,1)} %bitcast.93), kind=kOutput, calls=%fused_computation.193 | convolution fusion | flops 503316480 | bytes 21626880 | tf_op jit(solution)/shard_map/mgce,mel->mgcl/dot_general | solution.py:111
  626.9 5.8 fusion.48
  633.2 12.6 %all_to_all.52 = f32[16,16,2,256]{3,2,1,0:T(2,128)S(1)} all-to-all(f32[16,16,2,256]{3,2,1,0:T(2,128)S(1)} %copy.95), channel_id=1, replica_groups=mesh['chan'=16,'tm'=8] {'tm'}, dimensions={0} | all-to-all | bytes 1048576 | tf_op jit(solution)/shard_map/all_to_all | solution.py:116
  (80 shorter events, 103.6 us)
Async XLA Ops:
  4.6 169.6 %collective-permute-start = (bf16[16,15,4096]{2,0,1:T(8,128)(2,1)}, bf16[16,15,4096]{2,0,1:T(8,128)(2,1)}, u32[]{:S(2)}, u32[]{:S(2)}) collective-permute-start(bf16[16,15,4096]{2,0,1:T(8,128)(2,1)} %copy.103), channel_id=1, source_target_pairs={{0,1},{1,2},{2,3},{3,4},{4,5},{5,6},{6,7},{8,9},{9,10},{10,11},{11... | collective-permute-start | bytes 5898248 | tf_op jit(solution)/shard_map/ppermute | solution.py:15
  169.3 2.3 copy-start.7
  171.6 2.4 copy-start.10
  174.0 4.4 copy-start
  209.8 2.9 copy-start.9
  275.6 2.2 copy-start.1
  275.6 3.9 copy-start.2
  277.8 3.4 copy-start.3
  279.5 3.5 copy-start.4
  281.2 3.5 copy-start.5
  283.0 3.4 copy-start.6
  445.7 42.0 %all-to-all-start.1 = ((bf16[1,8,2,16,256,24]{4,5,3,2,0,1:T(8,128)(2,1)}), bf16[1,8,2,16,256,24]{4,5,3,2,0,1:T(8,128)(2,1)S(1)}, u32[]{:S(2)}, u32[]{:S(2)}) async-start(bf16[1,8,2,16,256,24]{4,5,3,2,0,1:T(8,128)(2,1)} %bitcast.97), calls=%async_computation.1 | async-start | bytes 6291456 | tf_op jit(solution)/shard_map/all_to_all | solution.py:81
  450.1 2.7 copy-start.11
  450.1 2.7 copy-start.12
  557.8 22.7 %copy-start.8 = (s32[120]{0:T(128)S(1)}, s32[120]{0:T(128)}, u32[]{:S(2)}) copy-start(s32[120]{0:T(128)} %constant.106) | copy-start | bytes 1444
where the time goes:
time: 658 us; the launch traced here: 647 us
  local copies, waits for them, and re-layouts  264 us (40%)
  other arithmetic  222 us (34%)
  matrix products  65.5 us (10%)
  blocking collectives  60.1 us (9%)
  waiting for transfers between devices  25.4 us (4%)
  starting transfers between devices  9.37 us (1%)
    convert_element_type x8, other arithmetic, body(): cosine = jnp.cos(phase_angle).astype(jnp.bfloat16)  145 us
    another operation x4, local copies, waits for them, and re-layouts, body(): jnp.stack([real_part, imag_part], axis=1)  65 us
    unnamed x36, local copies, waits for them, and re-layouts  63.9 us
    all_to_all x2, local copies, waits for them, and re-layouts, body(): lax.all_to_all(arranged, 'chan', split_axis=0, concat_axis=4, tiled=True)  62.5 us
    all_to_all x1, blocking collectives, body(): lax.all_to_all(arranged, 'chan', split_axis=0, concat_axis=4, tiled=True)  47.5 us
    dot_general x8, matrix products, body(): lax.dot_general(dft_table, rows_in, (((0,), (1,)), ((), ())), preferred_e...  42.9 us
    gather x2, local copies, waits for them, and re-layouts, body(): visibility = visibility[:, :, left_idx, :, right_idx, :]  30.6 us
    reshape x8, local copies, waits for them, and re-layouts, body(): spectrum.astype(jnp.bfloat16)  28.2 us
  transfers between devices with their start and end apart: 2, of which 1 were waited for; matrix products, arithmetic and copies ran while one was open for 27% of the time, Pallas kernels for 0%

commit v1 on v0

--- a/solution.py
+++ b/solution.py
@@ -113,7 +113,15 @@
     partial_value = jnp.einsum(
         "mgcl,ms->sgcl", per_block, slot_hits, precision=lax.Precision.HIGHEST
     )
-    uv_grid = lax.all_to_all(partial_value, "tm", split_axis=0, concat_axis=1, tiled=True)
+    ways, here = (lax.axis_size("tm"), lax.axis_index("tm"))
+    width = partial_value.shape[0] // ways
+    turned_2 = jnp.roll(partial_value, -here * width, axis=0)
+    got = [lax.slice_in_dim(turned_2, 0, width, axis=0)]
+    for far in range(1, ways):
+        sent = lax.slice_in_dim(turned_2, far * width, (far + 1) * width, axis=0)
+        got.append(lax.ppermute(sent, "tm", [(d, (d + far) % ways) for d in range(ways)]))
+    line = jnp.concatenate(got[::-1], axis=1)
+    uv_grid = jnp.roll(line, (here + 1) * got[0].shape[1], axis=1)
     return uv_grid
 
 

time: 658 us -> 658 us (level)
  blocking collectives: 60.1 us -> 47.4 us
  starting transfers between devices: 9.37 us -> 16.7 us
    all_to_all x1 -> x0, blocking collectives: 12.6 us -> none  [body(): lax.all_to_all(partial_value, 'tm', split_axis=0, concat_axis=1, tiled=True)]
    ppermute x0 -> x7, starting transfers between devices: none -> 7.31 us  [body(): lax.ppermute(sent, 'tm', [(d, (d + far) % ways) for d in range(ways)])]
    unnamed x36 -> x51, local copies, waits for them, and re-layouts: 63.9 us -> 64.1 us
  transfers between devices with their start and end apart: 2 -> 9, of which waited for: 1 -> 4; matrix products, arithmetic and copies ran while one was open for 27% -> 28% of each run, Pallas kernels for 0% -> 0%
where the time goes in v1:
time: 658 us; the launch traced here: 647 us
  local copies, waits for them, and re-layouts  267 us (41%)
  other arithmetic  225 us (34%)
  matrix products  65.5 us (10%)
  blocking collectives  47.4 us (7%)
  waiting for transfers between devices  25.4 us (4%)
  starting transfers between devices  16.7 us (3%)
    convert_element_type x8, other arithmetic, body(): cosine = jnp.cos(phase_angle).astype(jnp.bfloat16)  145 us
    another operation x4, local copies, waits for them, and re-layouts, body(): jnp.stack([real_part, imag_part], axis=1)  65.1 us
    unnamed x51, local copies, waits for them, and re-layouts  64.1 us
    all_to_all x2, local copies, waits for them, and re-layouts, body(): lax.all_to_all(arranged, 'chan', split_axis=0, concat_axis=4, tiled=True)  62.5 us
    all_to_all x1, blocking collectives, body(): lax.all_to_all(arranged, 'chan', split_axis=0, concat_axis=4, tiled=True)  47.4 us
    dot_general x8, matrix products, body(): lax.dot_general(dft_table, rows_in, (((0,), (1,)), ((), ())), preferred_e...  42.9 us
    gather x2, local copies, waits for them, and re-layouts, body(): visibility = visibility[:, :, left_idx, :, right_idx, :]  30.6 us
    reshape x8, local copies, waits for them, and re-layouts, body(): spectrum.astype(jnp.bfloat16)  28.2 us
  transfers between devices with their start and end apart: 9, of which 4 were waited for; matrix products, arithmetic and copies ran while one was open for 28% of the time, Pallas kernels for 0%

profile of v1, /device:TPU:1, one launch (start us, length us, event | category | flops | bytes accessed | tf_op | source)
XLA Modules:
  0.0 647.0 jit_solution(8940418722391289883)
XLA Ops:
  9.6 18.1 %cosine_convert_fusion.7 = (bf16[4096,16,1,16]{0,3,2,1:T(8,128)(2,1)S(1)}, bf16[4096,16,1,16]{0,3,2,1:T(8,128)(2,1)S(1)}) fusion(s32[16,16]{1,0:T(8,128)S(1)} %multiply_add_fusion), kind=kLoop, calls=%fused_computation.119 | loop fusion | flops 17825792 | bytes 4195328 | tf_op jit(solution)/shard_map/convert_element_type | solution.py:63
  27.7 18.1 %cosine_convert_fusion.6 = (bf16[4096,16,1,16]{0,3,2,1:T(8,128)(2,1)S(1)}, bf16[4096,16,1,16]{0,3,2,1:T(8,128)(2,1)S(1)}) fusion(s32[16,16]{1,0:T(8,128)S(1)} %fusion.85), kind=kLoop, calls=%fused_computation.115 | loop fusion | flops 17825792 | bytes 4195328 | tf_op jit(solution)/shard_map/convert_element_type | solution.py:63
  45.8 18.1 %cosine_convert_fusion.5 = (bf16[4096,16,1,16]{0,3,2,1:T(8,128)(2,1)S(1)}, bf16[4096,16,1,16]{0,3,2,1:T(8,128)(2,1)S(1)}) fusion(s32[16,16]{1,0:T(8,128)S(1)} %fusion.84), kind=kLoop, calls=%fused_computation.111 | loop fusion | flops 17825792 | bytes 4195328 | tf_op jit(solution)/shard_map/convert_element_type | solution.py:63
  63.9 18.1 %cosine_convert_fusion.4 = (bf16[4096,16,1,16]{0,3,2,1:T(8,128)(2,1)S(1)}, bf16[4096,16,1,16]{0,3,2,1:T(8,128)(2,1)S(1)}) fusion(s32[16,16]{1,0:T(8,128)S(1)} %fusion.83), kind=kLoop, calls=%fused_computation.107 | loop fusion | flops 17825792 | bytes 4195328 | tf_op jit(solution)/shard_map/convert_element_type | solution.py:63
  81.9 18.1 %cosine_convert_fusion.3 = (bf16[4096,16,1,16]{0,3,2,1:T(8,128)(2,1)S(1)}, bf16[4096,16,1,16]{0,3,2,1:T(8,128)(2,1)S(1)}) fusion(s32[16,16]{1,0:T(8,128)S(1)} %fusion.82), kind=kLoop, calls=%fused_computation.103 | loop fusion | flops 17825792 | bytes 4195328 | tf_op jit(solution)/shard_map/convert_element_type | solution.py:63
  100.0 18.1 %cosine_convert_fusion.2 = (bf16[4096,16,1,16]{0,3,2,1:T(8,128)(2,1)S(1)}, bf16[4096,16,1,16]{0,3,2,1:T(8,128)(2,1)S(1)}) fusion(s32[16,16]{1,0:T(8,128)S(1)} %fusion.81), kind=kLoop, calls=%fused_computation.99 | loop fusion | flops 17825792 | bytes 4195328 | tf_op jit(solution)/shard_map/convert_element_type | solution.py:63
  118.1 18.1 %cosine_convert_fusion.1 = (bf16[4096,16,1,16]{0,3,2,1:T(8,128)(2,1)S(1)}, bf16[4096,16,1,16]{0,3,2,1:T(8,128)(2,1)S(1)}) fusion(s32[16,16]{1,0:T(8,128)S(1)} %fusion.80), kind=kLoop, calls=%fused_computation.95 | loop fusion | flops 17825792 | bytes 4195328 | tf_op jit(solution)/shard_map/convert_element_type | solution.py:63
  136.2 19.0 %cosine_convert_fusion = (bf16[4096,16,1,16]{0,3,2,1:T(8,128)(2,1)S(1)}, bf16[4096,16,1,16]{0,3,2,1:T(8,128)(2,1)}) fusion(s32[16,16]{1,0:T(8,128)S(1)} %fusion.79), kind=kLoop, calls=%fused_computation.91 | loop fusion | flops 17825792 | bytes 4195328 | tf_op jit(solution)/shard_map/convert_element_type | solution.py:63
  178.4 23.2 %add_convert_fusion = bf16[16,24,4096]{2,1,0:T(8,128)(2,1)} fusion(bf16[16,24,4096]{2,1,0:T(8,128)(2,1)S(1)} %copy-done, bf16[16,15,4096]{2,1,0:T(8,128)(2,1)} %copy.79, f32[4096]{0:T(1024)S(1)} %bitcast.131, f32[4096]{0:T(1024)S(1)} %bitcast.132, f32[4096]{0:T(1024)S(1)} %bitcast.118, f32[4096]{0:T(1024)S(1)} %bitcast.119, f32[4096]{0:T(1024)S(1)} %bitcast.120, ...), kind=kLoop, calls=%fused_computation.52 | loop fusion | flops 146276352 | bytes 8519680 | tf_op jit(solution)/shard_map/convert_element_type | solution.py:51
  201.6 5.5 fusion.70
  220.2 5.5 fusion.72
  229.5 5.5 fusion.73
  238.7 5.5 fusion.74
  247.9 5.5 fusion.75
  257.3 5.5 fusion.76
  266.5 5.5 fusion.77
  288.2 22.6 %reshape.779 = bf16[16,2,49152]{2,1,0:T(2,128)(2,1)S(1)} reshape(bf16[16,8,2,16,16,24]{5,4,3,2,1,0:T(8,128)(2,1)} %bitcast.92) | data formatting | bytes 6291456
  310.9 47.4 %all_to_all.33 = bf16[16,2,49152]{2,1,0:T(2,128)(2,1)} all-to-all(bf16[16,2,49152]{2,1,0:T(2,128)(2,1)S(1)} %reshape.779), channel_id=1, replica_groups=mesh['chan'=16,'tm'=8] {'chan'}, dimensions={0} | all-to-all | bytes 6291456 | tf_op jit(solution)/shard_map/all_to_all | solution.py:82
  358.3 25.0 %reshape.780 = bf16[16,8,2,16,16,24]{5,4,3,2,1,0:T(8,128)(2,1)} reshape(bf16[16,2,49152]{2,1,0:T(2,128)(2,1)} %all_to_all.33) | data formatting | bytes 6291456
  383.3 32.4 %copy.80 = bf16[1,8,2,16,16,16,24]{5,4,6,3,2,1,0:T(8,128)(2,1)} copy(bf16[1,8,2,16,16,16,24]{6,5,3,2,1,4,0:T(8,128)(2,1)} %bitcast.88) | data formatting | bytes 6291456 | tf_op jit(solution)/shard_map/all_to_all | solution.py:82
  415.7 30.1 %all_to_all.27 = bf16[1,8,2,16,256,24]{4,5,3,2,1,0:T(8,128)(2,1)} reshape(bf16[1,8,2,16,16,16,24]{5,4,6,3,2,1,0:T(8,128)(2,1)} %copy.80) | data formatting | bytes 6291456 | tf_op jit(solution)/shard_map/all_to_all | solution.py:82
  458.2 8.6 %multiply_convert_fusion = bf16[120,256,16,16]{1,3,2,0:T(8,128)(2,1)} fusion(f32[120,256,16]{1,2,0:T(8,128)S(1)} %get-tuple-element.46, f32[120,256,16]{1,2,0:T(8,128)S(1)} %get-tuple-element.47), kind=kLoop, calls=%fused_computation.2 | loop fusion | flops 15728640 | bytes 19660800 | tf_op jit(solution)/shard_map/convert_element_type | solution.py:32
  466.9 20.9 %all-to-all-done.1 = bf16[1,8,2,16,256,24]{4,5,3,2,0,1:T(8,128)(2,1)S(1)} async-done(((bf16[1,8,2,16,256,24]{4,5,3,2,0,1:T(8,128)(2,1)}), bf16[1,8,2,16,256,24]{4,5,3,2,0,1:T(8,128)(2,1)S(1)}, u32[]{:S(2)}, u32[]{:S(2)}) %all-to-all-start.1) | async-done | bytes 3145760 | tf_op jit(solution)/shard_map/all_to_all | solution.py:81
  492.9 17.5 %stack.63 = bf16[16,1,16,16,16,16]{5,4,3,2,0,1:T(8,128)(2,1)} reshape(bf16[16,256,256]{2,1,0:T(8,128)(2,1)} %bitcast_multiply_fusion) | data formatting | bytes 4194304 | tf_op jit(solution)/shard_map/stack | solution.py:101
  510.3 16.6 %copy.86 = bf16[16,1,16,16,16,16]{5,3,4,2,1,0:T(8,128)(2,1)} copy(bf16[16,1,16,16,16,16]{5,4,3,2,0,1:T(8,128)(2,1)} %stack.63) | data formatting | bytes 4194304 | tf_op jit(solution)/shard_map/stack | solution.py:101
  527.0 14.4 %stack.61 = bf16[16,1,16,16,16,16]{5,4,3,2,0,1:T(8,128)(2,1)} reshape(bf16[16,256,256]{2,1,0:T(8,128)(2,1)S(1)} %bitcast_multiply_fusion.1) | data formatting | bytes 4194304 | tf_op jit(solution)/shard_map/stack | solution.py:101
  541.4 16.6 %copy.85 = bf16[16,1,16,16,16,16]{5,3,4,2,1,0:T(8,128)(2,1)} copy(bf16[16,1,16,16,16,16]{5,4,3,2,0,1:T(8,128)(2,1)} %stack.61) | data formatting | bytes 4194304 | tf_op jit(solution)/shard_map/stack | solution.py:101
  558.0 22.7 %pad_maximum_fusion = bf16[16,2,16,16,16,16]{5,3,4,2,1,0:T(8,128)(2,1)} fusion(bf16[16,1,16,16,16,16]{5,3,4,2,1,0:T(8,128)(2,1)} %copy.86, bf16[16,1,16,16,16,16]{5,3,4,2,1,0:T(8,128)(2,1)} %copy.85), kind=kLoop, calls=%fused_computation.1 | loop fusion | flops 2097152 | bytes 8388608 | tf_op jit(solution)/shard_map/stack | solution.py:101
  580.7 12.2 %gather_fusion = bf16[120,16,2,16,16]{4,3,2,1,0:T(8,128)(2,1)} fusion(bf16[16,2,16,16,16,16]{5,3,4,2,1,0:T(8,128)(2,1)} %pad_maximum_fusion, s32[120]{0:T(128)S(1)} %copy-done.8), kind=kCustom, calls=%fused_computation | custom fusion | bytes 3933120 | tf_op jit(solution)/shard_map/gather | solution.py:104
  592.9 18.3 %copy.87 = bf16[120,16,2,16,16]{0,4,3,2,1:T(8,128)(2,1)S(1)} copy(bf16[120,16,2,16,16]{4,3,2,1,0:T(8,128)(2,1)} %gather_fusion) | data formatting | bytes 3932160 | tf_op jit(solution)/shard_map/gather | solution.py:104
  614.5 12.6 %fusion.93 = f32[120,16,2,256]{3,1,2,0:T(8,128)} fusion(bf16[120,16,2,256]{3,1,2,0:T(8,128)(2,1)} %copy.90, bf16[120,256,256,1]{1,2,3,0:T(8,128)(2,1)} %bitcast.89), kind=kOutput, calls=%fused_computation.214 | convolution fusion | flops 503316480 | bytes 21626880 | tf_op jit(solution)/shard_map/mgce,mel->mgcl/dot_general | solution.py:111
  627.1 5.8 fusion.48
  (111 shorter events, 115.0 us)
Async XLA Ops:
  4.6 169.7 %collective-permute-start = (bf16[16,15,4096]{2,0,1:T(8,128)(2,1)}, bf16[16,15,4096]{2,0,1:T(8,128)(2,1)}, u32[]{:S(2)}, u32[]{:S(2)}) collective-permute-start(bf16[16,15,4096]{2,0,1:T(8,128)(2,1)} %copy.100), channel_id=1, source_target_pairs={{0,1},{1,2},{2,3},{3,4},{4,5},{5,6},{6,7},{8,9},{9,10},{10,11},{11... | collective-permute-start | bytes 5898248 | tf_op jit(solution)/shard_map/ppermute | solution.py:15
  169.3 2.3 copy-start.7
  171.7 2.4 copy-start.10
  174.0 4.4 copy-start
  209.9 2.9 copy-start.9
  275.7 2.2 copy-start.1
  275.7 3.9 copy-start.2
  277.9 3.5 copy-start.3
  279.7 3.5 copy-start.4
  281.4 3.5 copy-start.5
  283.1 3.4 copy-start.6
  445.8 42.0 %all-to-all-start.1 = ((bf16[1,8,2,16,256,24]{4,5,3,2,0,1:T(8,128)(2,1)}), bf16[1,8,2,16,256,24]{4,5,3,2,0,1:T(8,128)(2,1)S(1)}, u32[]{:S(2)}, u32[]{:S(2)}) async-start(bf16[1,8,2,16,256,24]{4,5,3,2,0,1:T(8,128)(2,1)} %bitcast.93), calls=%async_computation.1 | async-start | bytes 6291456 | tf_op jit(solution)/shard_map/all_to_all | solution.py:81
  450.2 5.3 copy-start.11
  450.2 5.3 copy-start.12
  558.0 22.7 %copy-start.8 = (s32[120]{0:T(128)S(1)}, s32[120]{0:T(128)}, u32[]{:S(2)}) copy-start(s32[120]{0:T(128)} %constant.154) | copy-start | bytes 1444
  633.3 6.5 %collective-permute-start.1 = (f32[2,16,2,256]{3,0,2,1:T(2,128)S(1)}, f32[2,16,2,256]{3,0,2,1:T(2,128)S(1)}, u32[]{:S(2)}, u32[]{:S(2)}) collective-permute-start(f32[2,16,2,256]{3,0,2,1:T(2,128)S(1)} %get-tuple-element.13), channel_id=1, source_target_pairs={{0,7},{1,0},{2,1},{3,2},{4,3},{5,4},{6,5},{7,6},{8,15},{9,8},{10,9... | collective-permute-start | bytes 196616 | tf_op jit(solution)/shard_map/ppermute | solution.py:122
  634.1 5.6 collective-permute-start.2
  635.0 5.6 collective-permute-start.3
  636.2 4.7 collective-permute-start.4
  638.0 5.8 collective-permute-start.5
  639.8 5.3 collective-permute-start.6
  639.8 5.3 collective-permute-start.7
